TPU v7x, 256 devices: a whole 4x4x8 slice. The times are simulated.
256 devices in a mesh: ep: 64 (over x, z, y_hi), tp: 4 (over y_lo, core).
Axes of the slice: x: 4, y: 4 (y_hi: 2, y_lo: 2; y = y_hi * 2 + y_lo), z: 8, core: 2. Of those that a mesh axis runs over, the one named last changes fastest.
Arguments:
- tokens: bfloat16 [1024, 7168], P('ep', 'tp'), may hold values from -6 to 6
- expert_ids: int32 [1024, 8], P('ep'), may hold values from 0 to 63, all different within a row; in each aligned block of 16 rows (0 to 15, 16 to 31, ...) at most 4 rows name the same one
- gate_weights: float32 [1024, 8], P('ep'), may hold values from 0.1 to 1
- expert_gate_up: bfloat16 [64, 7168, 2, 1024], P('ep', None, None, 'tp'), may hold values from -0.0625 to 0.0625
- expert_down: bfloat16 [64, 7168, 1024], P('ep', None, 'tp'), may hold values from -0.1875 to 0.1875
- queries: bfloat16 [1024, 64, 576], P('ep', 'tp'), may hold values from -8 to 8
- latent_cache: bfloat16 [3072, 16, 576], P('ep'), may hold values from -8 to 8
- block_source: int32 [3072], replicated, may hold values from 0 to 3071, as said below
- block_request: int32 [3072], P('ep'), may hold values from -1 to 15, as said below
- block_used: int32 [3072], P('ep'), may hold values from 0 to 16, as said below
Outputs:
- moe_out: bfloat16 [1024, 7168], P('ep', 'tp')
- attention_out: bfloat16 [1024, 64, 512], P('ep', 'tp')
Inputs may be any that keep to these rules, and one draw needn't show every extreme that they name: `expert_ids`: each row names 8 different experts; among the rows of one index of ep no expert is named by more than 4 rows, a bound that some block reaches. `block_source`: A permutation. `block_request`: within one index of ep each row holds a run of 1 to 3 consecutive slots, rows in order from the first slot, unused slots (-1) after them; some index of ep holds 3 slots for every row, and some has unused slots. `block_used`: 16 in every used slot but a row's last one, which holds 2 to 16; 0 in unused slots.
All inputs are finite; a program needn't handle non-finite values.
Results may differ from a plain program's by a relative error of at most 0.015.
Values may be sent and summed in bfloat16 or wider, within the bound.
A program may use at most 64 MiB of HBM per device.

v0:
```python
import jax
import jax.numpy as jnp
from jax import lax
from jax.sharding import PartitionSpec as P

KV = 512


score_scale = 192.0 ** (-0.5)


def move_blocks(flat_cache, block_source):
    spread = lax.all_to_all(flat_cache, "ep", split_axis=1, concat_axis=0, tiled=True)
    ordered = jnp.take(spread, block_source, axis=0)
    return lax.all_to_all(ordered, "ep", split_axis=0, concat_axis=1, tiled=True)


def body(
    tokens,
    expert_ids,
    gate_weights,
    expert_gate_up,
    expert_down,
    queries,
    latent_cache,
    block_source,
    block_request,
    block_used,
):
    row_count, top_count = expert_ids.shape
    ep_size = lax.axis_size("ep")
    capacity = min(row_count, max(2, 2 * row_count * top_count // ep_size))
    slot_count = ep_size * capacity
    expert_range = jnp.arange(ep_size, dtype=jnp.int32)
    flat_destination = expert_ids.reshape(-1)
    device_hot = (flat_destination[:, None] == expert_range[None, :]).astype(jnp.int32)
    position = jnp.sum((jnp.cumsum(device_hot, axis=0) - device_hot) * device_hot, axis=1)
    slot_of = flat_destination * capacity + position
    placed = slot_of[:, None] == jnp.arange(slot_count, dtype=jnp.int32)[None, :]
    row_place = jnp.any(placed.reshape(row_count, top_count, slot_count), axis=1).astype(
        jnp.bfloat16
    )
    weight_place = jnp.sum(
        jnp.where(placed, gate_weights.reshape(-1)[:, None], 0.0).reshape(
            row_count, top_count, slot_count
        ),
        axis=1,
    )
    contract_rows = (((0,), (0,)), ((), ()))
    full_rows = lax.all_gather(tokens, "tp", axis=1, tiled=True)
    outgoing = lax.dot_general(
        row_place, full_rows, contract_rows, preferred_element_type=jnp.float32
    ).astype(jnp.bfloat16)
    arrived = lax.all_to_all(
        outgoing.reshape(ep_size, capacity, -1), "ep", split_axis=0, concat_axis=0, tiled=True
    )
    slot_rows = arrived.reshape(slot_count, -1)
    gate_and_up = jnp.einsum(
        "sd,dgf->sgf", slot_rows, expert_gate_up[0], preferred_element_type=jnp.float32
    )
    hidden = (jax.nn.silu(gate_and_up[:, 0]) * gate_and_up[:, 1]).astype(jnp.bfloat16)
    partial_value = lax.dot_general(
        hidden, expert_down[0], (((1,), (1,)), ((), ())), preferred_element_type=jnp.float32
    )
    summed = lax.psum_scatter(
        partial_value.astype(jnp.bfloat16), "tp", scatter_dimension=1, tiled=True
    )
    returned = lax.all_to_all(
        summed.reshape(ep_size, capacity, -1), "ep", split_axis=0, concat_axis=0, tiled=True
    )
    returned_rows = returned.reshape(slot_count, -1).astype(jnp.float32)
    moe_out = jnp.dot(
        weight_place,
        returned_rows,
        precision=lax.Precision.HIGHEST,
        preferred_element_type=jnp.float32,
    ).astype(jnp.bfloat16)
    slot_total, block_size, latent = latent_cache.shape
    flat_cache = latent_cache.reshape(slot_total, block_size * latent)
    cache_now = move_blocks(flat_cache, block_source)
    key_rows = cache_now.reshape(slot_total * block_size, latent)
    owner_token = jnp.repeat(block_request, block_size)
    limit_token = jnp.repeat(block_used, block_size)
    within = jnp.tile(jnp.arange(block_size, dtype=jnp.int32), slot_total)
    visible = (owner_token[None, :] == jnp.arange(row_count, dtype=jnp.int32)[:, None]) & (
        within < limit_token
    )[None, :]
    scores = (
        jnp.einsum("rhc,tc->rht", queries, key_rows, preferred_element_type=jnp.float32)
        * score_scale
    )
    scores = jnp.where(visible[:, None, :], scores, -jnp.inf)
    row_max = jnp.max(scores, axis=2, keepdims=True)
    exponent_terms = jnp.exp(scores - row_max)
    weights = (exponent_terms / jnp.sum(exponent_terms, axis=2, keepdims=True)).astype(jnp.bfloat16)
    attended = jnp.einsum(
        "rht,tc->rhc", weights, key_rows[:, :KV], preferred_element_type=jnp.float32
    ).astype(jnp.bfloat16)
    return (moe_out, attended)


def solution(mesh):
    placed = (
        P("ep", "tp"),
        P("ep", None),
        P("ep", None),
        P("ep", None, None, "tp"),
        P("ep", None, "tp"),
        P("ep", "tp", None),
        P("ep", None, None),
        P(),
        P("ep"),
        P("ep"),
    )
    return jax.shard_map(
        body,
        mesh=mesh,
        in_specs=placed,
        out_specs=(P("ep", "tp"), P("ep", "tp", None)),
        check_vma=False,
    )
```

profile of v0, /device:TPU:1, one launch (start us, length us, event | category | flops | bytes accessed | tf_op | source)
XLA Modules:
  0.0 295.4 jit_solution(11487443691566335392)
XLA Ops:
  7.2 0.0 copy-start
  7.2 0.0 reduce-scatter.2.cloned.1.call-start
  7.2 0.8 copy.33
  8.0 0.1 eq.49
  8.1 0.1 fusion.14
  8.2 0.2 reduce_window_sum.11
  8.4 0.2 select_reduce_fusion.1
  8.6 0.1 reduce_sum.30
  8.7 0.1 fusion.13
  8.8 9.0 %all_gather.3 = bf16[16,7168]{1,0:T(8,128)(2,1)S(1)} all-gather(bf16[16,1792]{1,0:T(8,128)(2,1)} %param.10), channel_id=1, replica_groups=mesh['ep'=64,'tp'=4] {'tp'}, dimensions={1}, use_global_device_ids=true | all-gather | bytes 286720 | tf_op jit(solution)/shard_map/all_gather | solution.py:50
  17.8 3.0 %convolution_convert_fusion.1 = bf16[256,7168]{1,0:T(8,128)(2,1)} fusion(pred[16,256]{1,0:T(8,128)(4,1)S(1)} %fusion.13, bf16[16,7168]{1,0:T(8,128)(2,1)S(1)} %all_gather.3), kind=kOutput, calls=%fused_computation.3 | convolution fusion | flops 60555264 | bytes 3903488 | tf_op jit(solution)/shard_map/dot_general | solution.py:51
  20.8 7.0 %reshape.119 = bf16[64,4,7168]{2,1,0:T(4,128)(2,1)} reshape(bf16[256,7168]{1,0:T(8,128)(2,1)} %convolution_convert_fusion.1) | data formatting | bytes 7340032 | tf_op jit(solution)/shard_map/reshape | solution.py:55
  27.8 97.8 %all_to_all.42 = bf16[64,4,7168]{2,1,0:T(4,128)(2,1)} all-to-all(bf16[64,4,7168]{2,1,0:T(4,128)(2,1)} %reshape.119), channel_id=1, replica_groups=mesh['ep'=64,'tp'=4] {'ep'}, dimensions={0} | all-to-all | bytes 7340032 | tf_op jit(solution)/shard_map/all_to_all | solution.py:54
  125.6 6.7 %reshape.133 = bf16[256,7168,1]{1,0,2:T(8,128)(2,1)} reshape(bf16[64,4,7168]{2,1,0:T(4,128)(2,1)} %all_to_all.42) | data formatting | bytes 7340032 | tf_op jit(solution)/shard_map/reshape | solution.py:57
  132.4 6.4 %fusion.1 = f32[256,2,256]{2,0,1:T(8,128)S(1)} fusion(bf16[256,7168,1]{1,0,2:T(8,128)(2,1)} %reshape.133, bf16[7168,2,256]{2,1,0:T(2,128)(2,1)} %bitcast.33), kind=kOutput, calls=%fused_computation.4 | convolution fusion | flops 1879048192 | bytes 11534336 | tf_op jit(solution)/shard_map/sd,dgf->sgf/dot_general | solution.py:58
  138.8 3.0 %convolution_convert_fusion = bf16[256,7168]{1,0:T(8,128)(2,1)} fusion(bf16[1,7168,256]{2,1,0:T(8,128)(2,1)S(1)} %copy-done.1, f32[256,2,256]{2,0,1:T(8,128)S(1)} %fusion.1), kind=kOutput, calls=%fused_computation.2 | convolution fusion | flops 941752320 | bytes 7864320 | tf_op jit(solution)/shard_map/dot_general | solution.py:62
  141.7 0.0 reduce-scatter.2.cloned.1.call-update
  141.7 1.2 copy-done.2
  142.9 1.3 all_to_all.32
  144.3 0.0 copy-start.3
  144.3 2.1 copy.37
  146.3 7.0 %all-to-all-start.2 = ((bf16[48,64,144]{2,0,1:T(8,128)(2,1)}), bf16[48,64,144]{2,0,1:T(8,128)(2,1)S(1)}, u32[]{:S(2)}, u32[]{:S(2)}) async-start(bf16[48,64,144]{2,0,1:T(8,128)(2,1)} %copy.37), calls=%async_computation.3 | async-start | bytes 3145728 | tf_op jit(solution)/shard_map/all_to_all | solution.py:13
  153.3 0.0 copy-done.3
  153.4 0.1 broadcast_in_dim.57
  153.5 39.4 %all-to-all-done.2 = bf16[48,64,144]{2,0,1:T(8,128)(2,1)S(1)} async-done(((bf16[48,64,144]{2,0,1:T(8,128)(2,1)}), bf16[48,64,144]{2,0,1:T(8,128)(2,1)S(1)}, u32[]{:S(2)}, u32[]{:S(2)}) %all-to-all-start.2) | async-done | bytes 884768 | tf_op jit(solution)/shard_map/all_to_all | solution.py:13
  192.9 11.1 %gather_fusion = bf16[3072,144]{1,0:T(8,128)(2,1)S(1)} fusion(bf16[3072,144]{1,0:T(8,128)(2,1)S(1)} %bitcast.30, s32[3072]{0:T(1024)S(1)} %fusion.16), kind=kCustom, calls=%fused_computation | custom fusion | bytes 1781760 | tf_op jit(solution)/shard_map/jit(_take)/gather | solution.py:14
  204.0 1.5 broadcast_select_fusion
  205.4 7.6 %all-to-all-start.3 = ((bf16[64,48,144]{2,1,0:T(8,128)(2,1)}), bf16[64,48,144]{2,1,0:T(8,128)(2,1)S(1)}, u32[]{:S(2)}, u32[]{:S(2)}) async-start(bf16[64,48,144]{2,1,0:T(8,128)(2,1)} %broadcast_select_fusion), calls=%async_computation.4 | async-start | bytes 3145728 | tf_op jit(solution)/shard_map/all_to_all | solution.py:15
  213.0 0.0 reduce-scatter.2.cloned.1.call-done
  213.1 2.5 reshape.121
  215.6 36.5 %all-to-all-done.3 = bf16[64,48,144]{2,1,0:T(8,128)(2,1)S(1)} async-done(((bf16[64,48,144]{2,1,0:T(8,128)(2,1)}), bf16[64,48,144]{2,1,0:T(8,128)(2,1)S(1)}, u32[]{:S(2)}, u32[]{:S(2)}) %all-to-all-start.3) | async-done | bytes 884768 | tf_op jit(solution)/shard_map/all_to_all | solution.py:15
  252.2 8.3 %all-to-all-start.1 = ((bf16[64,4,1792]{2,1,0:T(4,128)(2,1)}), bf16[64,4,1792]{2,1,0:T(4,128)(2,1)}, u32[]{:S(2)}, u32[]{:S(2)}) async-start(bf16[64,4,1792]{2,1,0:T(4,128)(2,1)} %reshape.121), calls=%async_computation.2 | async-start | bytes 1835008 | tf_op jit(solution)/shard_map/all_to_all | solution.py:68
  260.5 0.1 copy.35
  260.6 0.0 copy-done.5
  260.6 0.1 broadcast_in_dim.54
  260.6 0.1 eq.56
  260.7 0.0 copy-done.6
  260.7 0.1 iota_compare_fusion.3
  260.8 0.1 lt.19
  260.9 0.1 select_reduce_fusion
  261.1 0.5 copy.38
  261.6 2.4 reshape.123
  264.0 0.5 fusion.7
  264.5 0.3 fusion.19
  264.8 1.5 convolution_convert_fusion.3
  266.3 19.5 %all-to-all-done.1 = bf16[64,4,1792]{2,1,0:T(4,128)(2,1)} async-done(((bf16[64,4,1792]{2,1,0:T(4,128)(2,1)}), bf16[64,4,1792]{2,1,0:T(4,128)(2,1)}, u32[]{:S(2)}, u32[]{:S(2)}) %all-to-all-start.1) | async-done | bytes 917536 | tf_op jit(solution)/shard_map/all_to_all | solution.py:68
  285.7 1.6 reshape.122
  287.4 1.1 convolution_convert_fusion.2
  (12 shorter events, 0.1 us)
Async XLA Ops:
  7.2 256.8 %copy-start = (bf16[16,16,576]{2,1,0:T(8,128)(2,1)S(1)}, bf16[16,16,576]{2,1,0:T(8,128)(2,1)}, u32[]{:S(2)}) copy-start(bf16[16,16,576]{2,1,0:T(8,128)(2,1)} %param.15) | copy-start | bytes 884740
  7.2 205.9 %reduce-scatter.2.cloned.1.call-start = ((), (), s32[]{:S(2)}) async-start(), calls=%async_computation.5 | async-start | bytes 4587520 | tf_op jit(solution)/shard_map/reduce_scatter | solution.py:65
  132.4 6.4 %copy-start.1 = (bf16[1,7168,256]{2,1,0:T(8,128)(2,1)S(1)}, bf16[1,7168,256]{2,1,0:T(8,128)(2,1)}, u32[]{:S(2)}) copy-start(bf16[1,7168,256]{2,1,0:T(8,128)(2,1)} %param.14) | copy-start | bytes 11010052
  141.7 1.2 copy-start.2
  144.3 9.1 %copy-start.3 = (s32[3072]{0:T(1024)S(1)}, s32[3072]{0:T(1024)}, u32[]{:S(2)}) copy-start(s32[3072]{0:T(1024)} %param.17) | copy-start | bytes 36868
  146.3 46.6 %all-to-all-start.2 = ((bf16[48,64,144]{2,0,1:T(8,128)(2,1)}), bf16[48,64,144]{2,0,1:T(8,128)(2,1)S(1)}, u32[]{:S(2)}, u32[]{:S(2)}) async-start(bf16[48,64,144]{2,0,1:T(8,128)(2,1)} %copy.37), calls=%async_computation.3 | async-start | bytes 3145728 | tf_op jit(solution)/shard_map/all_to_all | solution.py:13
  205.4 55.0 %copy-start.4 = (f32[16,8]{0,1:T(8,128)S(1)}, f32[16,8]{0,1:T(8,128)}, u32[]{:S(2)}) copy-start(f32[16,8]{0,1:T(8,128)} %param.12) | copy-start | bytes 1540
  205.4 55.1 %copy-start.5 = (s32[48]{0:T(128)S(1)}, s32[48]{0:T(128)}, u32[]{:S(2)}) copy-start(s32[48]{0:T(128)} %param.18) | copy-start | bytes 580
  205.4 55.3 %copy-start.6 = (s32[48]{0:T(128)S(1)}, s32[48]{0:T(128)}, u32[]{:S(2)}) copy-start(s32[48]{0:T(128)} %param.19) | copy-start | bytes 580
  205.4 46.7 %all-to-all-start.3 = ((bf16[64,48,144]{2,1,0:T(8,128)(2,1)}), bf16[64,48,144]{2,1,0:T(8,128)(2,1)S(1)}, u32[]{:S(2)}, u32[]{:S(2)}) async-start(bf16[64,48,144]{2,1,0:T(8,128)(2,1)} %broadcast_select_fusion), calls=%async_computation.4 | async-start | bytes 3145728 | tf_op jit(solution)/shard_map/all_to_all | solution.py:15
  252.2 33.6 %all-to-all-start.1 = ((bf16[64,4,1792]{2,1,0:T(4,128)(2,1)}), bf16[64,4,1792]{2,1,0:T(4,128)(2,1)}, u32[]{:S(2)}, u32[]{:S(2)}) async-start(bf16[64,4,1792]{2,1,0:T(4,128)(2,1)} %reshape.121), calls=%async_computation.2 | async-start | bytes 1835008 | tf_op jit(solution)/shard_map/all_to_all | solution.py:68
Sparse Core Ops, SparseCore 0:
  141.9 56.7 reduce-scatter.1
where the time goes:
time: 297 us; the launch traced here: 295 us
  blocking collectives  107 us (36%)
  waiting for transfers between devices  95.5 us (32%)
  local copies, waits for them, and re-layouts  37.9 us (13%)
  starting transfers between devices  23 us (8%)
  matrix products  15.4 us (5%)
  between operations  14.2 us (5%)
    all_to_all x1, blocking collectives, body(): lax.all_to_all(outgoing.reshape(ep_size, capacity, -1), 'ep', split_axis=...  97.8 us
    all_to_all x1, waiting for transfers between devices, move_blocks(): lax.all_to_all(flat_cache, 'ep', split_axis=1, concat_axis=0, tiled=True)  39.4 us
    all_to_all x1, waiting for transfers between devices, move_blocks(): lax.all_to_all(ordered, 'ep', split_axis=0, concat_axis=1, tiled=True)  36.5 us
    all_to_all x1, waiting for transfers between devices, body(): lax.all_to_all(summed.reshape(ep_size, capacity, -1), 'ep', split_axis=0,...  19.5 us
    gather x1, local copies, waits for them, and re-layouts, move_blocks(): ordered = jnp.take(spread, block_source, axis=0)  11.1 us
    all_gather x1, blocking collectives, body(): full_rows = lax.all_gather(tokens, 'tp', axis=1, tiled=True)  8.98 us
    all_to_all x1, starting transfers between devices, body(): lax.all_to_all(summed.reshape(ep_size, capacity, -1), 'ep', split_axis=0,...  8.32 us
    all_to_all x1, starting transfers between devices, move_blocks(): lax.all_to_all(ordered, 'ep', split_axis=0, concat_axis=1, tiled=True)  7.59 us
  transfers between devices with their start and end apart: 4, of which 3 were waited for; matrix products, arithmetic and copies ran while one was open for 8% of the time, Pallas kernels for 0%

commit v1 on v0

v1 whole, which is shorter than its diff:
```python
import jax
import jax.numpy as jnp
from jax import lax
from jax.experimental import pallas as pl
from jax.experimental.pallas import tpu as pltpu
from jax.sharding import PartitionSpec as P

MESH = pl.DeviceIdType.MESH

D = 7168
QF = 1792
HID = 256
ROWS = 16
NX, NZ = 4, 8
CAP = 4
SLOTS = 48
BLK = 16
LAT = 576
KV = 512
PART = 384
KL = 2 * PART
ORDER = (0, 1, 3, 2)

score_scale = 192.0 ** (-0.5)


def place():
    ep, tp = lax.axis_index("ep"), lax.axis_index("tp")
    x = lax.div(ep, 16)
    z = lax.rem(lax.div(ep, 2), NZ)
    return x, z, lax.rem(ep, 2), lax.div(tp, 2), lax.rem(tp, 2)


def device(x, z, yh, yl, c):
    return ((x * NZ + z) * 2 + yh, yl * 2 + c)


class Copies:
    def __init__(self, send, recv):
        self.send, self.recv, self.made, self.count = send, recv, {}, 0

    def start(self, name, src, dst, to):
        i = self.count
        self.count += 1
        copy = pltpu.make_async_remote_copy(
            src_ref=src,
            dst_ref=dst,
            send_sem=self.send.at[i],
            recv_sem=self.recv.at[i],
            device_id=to,
            device_id_type=MESH,
        )
        copy.start()
        self.made[name] = copy

    def arrived(self, name):
        self.made[name].wait_recv()

    def finish(self):
        for copy in self.made.values():
            copy.wait_send()


def kernel(
    meta_ref,
    tok_ref,
    cq_ref,
    jb_ref,
    q_ref,
    mask_ref,
    wgu_ref,
    wd_ref,
    moe_ref,
    att_ref,
    send_sem,
    recv_sem,
    local_sem,
    wgu,
    wd,
    metag,
    meta_t,
    rows,
    selw,
    xsend,
    slots,
    other,
    part,
    mate,
    chip,
    back,
    ebuf,
    bbuf,
    zsend,
    zrecv,
    cz,
    cxs,
    cxr,
    cm,
    keys,
    qp,
):
    x, z, yh, yl, c = place()
    tp = yl * 2 + c
    group = lax.rem(yl + yh, 2)
    copies = Copies(send_sem, recv_sem)

    def at_x(e):
        return device(lax.rem(x + e, NX), z, yh, yl, c)

    def at_z(d):
        return device(x, lax.rem(z + d, NZ), yh, yl, c)

    core = device(x, z, yh, yl, 1 - c)
    near = device(x, z, yh, 1 - yl, c)
    cross = device(x, z, 1 - yh, 1 - yl, c)
    far = device(x, z, 1 - yh, yl, c)

    wgu_copy = pltpu.make_async_copy(wgu_ref, wgu, local_sem.at[0])
    wd_copy = pltpu.make_async_copy(wd_ref, wd, local_sem.at[1])
    wgu_copy.start()
    wd_copy.start()

    barrier = pltpu.get_barrier_semaphore()
    partners = [at_x(e) for e in range(1, NX)] + [at_z(d) for d in range(1, NZ)]
    partners += [core, near, cross, far]
    for partner in partners:
        pl.semaphore_signal(barrier, inc=1, device_id=partner, device_id_type=MESH)
    pl.semaphore_wait(barrier, len(partners))

    far_first = (1, 7, 2, 6, 3, 5, 4)
    for d in far_first:
        copies.start(("meta", d), meta_ref, metag.at[d], at_z(d))
    for d in far_first:
        copies.start(("tok", d), tok_ref, rows.at[pl.ds(d * ROWS, ROWS)], at_z(d))

    def piece(d):
        to = lax.rem(z + d, NZ)
        lane = pl.multiple_of(lax.rem(to, 2) * 256, 256)
        return cq_ref.at[lax.div(to, 2), :, pl.ds(lane, PART)]

    own_piece = pltpu.make_async_copy(piece(0), cz.at[pl.ds(0, SLOTS)], local_sem.at[2])
    own_piece.start()
    for d in far_first:
        copies.start(("cz", d), piece(d), cz.at[pl.ds(d * SLOTS, SLOTS)], at_z(d))

    metag[0] = meta_ref[...]
    rows[0:ROWS] = tok_ref[...]
    for d in far_first:
        copies.arrived(("meta", d))
    meta_t[...] = metag[...].reshape(NZ * ROWS, 128).T

    slot_at = lax.broadcasted_iota(jnp.int32, (32, 128), 0)
    row_at = lax.broadcasted_iota(jnp.int32, (32, 128), 1)
    same_source = lax.shift_right_logical(slot_at, 2) == lax.shift_right_logical(row_at, 4)
    slot_rank = lax.bitwise_and(slot_at, 3).astype(jnp.float32)

    def chosen(e, rel):
        at = z * 8 + lax.rem(x + e, NX) * 2 + (yh if rel == 0 else 1 - yh)
        code = meta_t[pl.ds(at, 1), :]
        weight = meta_t[pl.ds(at + 64, 1), :]
        hot = same_source & (slot_rank == code)
        selw[pl.ds(e * 64 + rel * 32, 32), :] = jnp.where(hot, weight, 0.0)
        return jnp.where(hot, 1.0, 0.0).astype(jnp.bfloat16)

    picks = {}
    for e in ORDER:
        picks[e] = jnp.concatenate([chosen(e, 0), chosen(e, 1)], axis=0)
    for d in far_first:
        copies.arrived(("tok", d))

    def own_rows(e):
        return pl.ds(e * 64, 32)

    def other_rows(e):
        return pl.ds(e * 64 + 32, 32)

    def pick(e):
        return jnp.dot(picks[e], rows[...], preferred_element_type=jnp.float32).astype(jnp.bfloat16)

    def along_y(e):
        copies.start(("near", e), slots.at[tp, own_rows(e)], slots.at[tp, own_rows(e)], near)
        copies.start(("cross", e), other.at[e], slots.at[tp, other_rows(e)], cross)
        copies.start(("far", e), other.at[e], slots.at[tp, other_rows(e)], far)

    picked = pick(0)
    slots[tp, 0:32] = picked[:32]
    other[0] = picked[32:]
    along_y(0)
    for e in (1, 3, 2):
        xsend[e] = pick(e)
        copies.start(("x0", e), xsend.at[e, pl.ds(0, 32)], slots.at[tp, own_rows(e)], at_x(e))
        copies.start(("x1", e), xsend.at[e, pl.ds(32, 32)], other.at[e], at_x(e))

    def from_x(e):
        copies.arrived(("x0", e))
        copies.arrived(("x1", e))
        along_y(e)

    near_tp = (1 - yl) * 2 + c

    def to_core(e):
        whole = pl.ds(e * 64, 64)
        copies.arrived(("near", e))
        copies.arrived(("cross", e))
        copies.start(("core_n", e), slots.at[near_tp, whole], slots.at[near_tp, whole], core)
        copies.arrived(("far", e))
        copies.start(("core_o", e), slots.at[tp, whole], slots.at[tp, whole], core)

    def expert(e):
        copies.arrived(("core_n", e))
        copies.arrived(("core_o", e))

        def add(k, total):
            at = pl.multiple_of(k * QF, 256)
            return total + jnp.dot(
                slots[k, pl.ds(e * 64, 64), :],
                wgu[pl.ds(at, QF), :],
                preferred_element_type=jnp.float32,
            )

        both = lax.fori_loop(0, 4, add, jnp.zeros((64, 2 * HID), jnp.float32))
        gate, up = both[:, :HID], both[:, HID:]
        hidden = (gate / (1.0 + jnp.exp(-gate)) * up).astype(jnp.bfloat16)

        @pl.loop(0, 4)
        def down(k):
            at = pl.multiple_of(k * QF, 256)
            part[e, lax.rem(k, 2), lax.div(k, 2)] = lax.dot_general(
                hidden,
                wd[pl.ds(at, QF), :],
                (((1,), (1,)), ((), ())),
                preferred_element_type=jnp.float32,
            ).astype(jnp.bfloat16)

        copies.start(("mate", e), part.at[e, 1 - c], mate.at[e], core)

    def chip_sum(e):
        copies.arrived(("mate", e))
        for h in range(2):
            chip[e, h] = (
                part[e, c, h].astype(jnp.float32) + mate[e, h].astype(jnp.float32)
            ).astype(jnp.bfloat16)
        low, high = pl.ds(0, 32), pl.ds(32, 32)
        copies.start(("r_near", e), chip.at[e, 1 - yl, low], back.at[e, 0], near)
        copies.start(("r_cross", e), chip.at[e, 1 - yl, high], back.at[e, 1], cross)
        copies.start(("r_far", e), chip.at[e, yl, high], back.at[e, 2], far)

    def expert_out(e):
        into = bbuf if e == 0 else ebuf
        copies.arrived(("r_near", e))
        into[e, 0:32] = (
            chip[e, yl, 0:32].astype(jnp.float32) + back[e, 0].astype(jnp.float32)
        ).astype(jnp.bfloat16)
        copies.arrived(("r_cross", e))
        copies.arrived(("r_far", e))
        into[e, 32:64] = (
            back[e, 1].astype(jnp.float32) + back[e, 2].astype(jnp.float32)
        ).astype(jnp.bfloat16)
        if e != 0:
            copies.start(("r_x", e), ebuf.at[e], bbuf.at[e], at_x(NX - e))

    def cache_swap():
        own_piece.wait()
        for d in far_first:
            copies.arrived(("cz", d))
        half = NZ * SLOTS
        copies.start(("swap", 0), cz.at[pl.ds(0, half)], cz.at[pl.ds(half, half)], cross)

    def cache_pick():
        copies.arrived(("swap", 0))
        lanes = lax.broadcasted_iota(jnp.int32, (NZ * SLOTS, 128), 1)
        for e in (2, 1, 3, 0):
            at = pl.multiple_of(lax.rem(x + e, NX) * (NZ * SLOTS), 128)
            wanted = jb_ref[pl.ds(at, NZ * SLOTS), :]
            hot = jnp.concatenate(
                [
                    jnp.where(wanted == lanes + 128 * k, 1.0, 0.0).astype(jnp.bfloat16)
                    for k in range(6)
                ],
                axis=1,
            )
            found = jnp.dot(hot, cz[...], preferred_element_type=jnp.float32).astype(jnp.bfloat16)
            if e == 0:
                cxr[0] = found
            else:
                cxs[e] = found
                copies.start(("cx", e), cxs.at[e], cxr.at[e], at_x(e))

    local = {}

    def cache_merge():
        for e in (1, 3, 2):
            copies.arrived(("cx", e))
        cm[...] = (cxr[0] + cxr[1]) + (cxr[2] + cxr[3])
        lane = pl.multiple_of(lax.rem(z, 2) * PART, 128)
        landing = keys.at[group, c, lax.div(z, 2), :, pl.ds(lane, PART)]

        def of(d):
            at = pl.multiple_of(lax.rem(z + d, NZ) * SLOTS, 16)
            return cm.at[pl.ds(at, SLOTS)]

        local["k"] = pltpu.make_async_copy(of(0), landing, local_sem.at[3])
        local["k"].start()
        for d in far_first:
            copies.start(("k", d), of(d), landing, at_z(d))

    def cache_tp():
        local["k"].wait()
        for d in far_first:
            copies.arrived(("k", d))
        copies.start(("k_near", 0), keys.at[group, c], keys.at[group, c], near)
        copies.start(("k_core", 0), keys.at[group, c], keys.at[group, c], core)

    def cache_core():
        copies.arrived(("k_near", 0))
        copies.start(("k_core", 1), keys.at[1 - group, c], keys.at[1 - group, c], core)

    def attention():
        copies.arrived(("k_core", 0))
        copies.arrived(("k_core", 1))
        qp[...] = jnp.zeros_like(qp)
        qp[:, 0:256] = q_ref[:, 0:256]
        qp[:, PART : PART + LAT - 256] = q_ref[:, 256:LAT]
        held = keys[...].reshape(SLOTS * BLK, KL)
        scores = (
            lax.dot_general(
                qp[...], held, (((1,), (1,)), ((), ())), preferred_element_type=jnp.float32
            )
            * score_scale
        )
        seen = jnp.broadcast_to(mask_ref[...][:, None, :], (ROWS, 16, SLOTS * BLK)).reshape(
            256, SLOTS * BLK
        )
        scores = jnp.where(seen > 0.0, scores, -1e30)
        terms = jnp.exp(scores - jnp.max(scores, axis=1, keepdims=True))
        weights = (terms / jnp.sum(terms, axis=1, keepdims=True)).astype(jnp.bfloat16)
        att_ref[:, 0:256] = jnp.dot(
            weights, held[:, 0:256], preferred_element_type=jnp.float32
        ).astype(jnp.bfloat16)
        att_ref[:, 256:KV] = jnp.dot(
            weights, held[:, PART : PART + 256], preferred_element_type=jnp.float32
        ).astype(jnp.bfloat16)

    cache_swap()
    from_x(1)
    to_core(0)
    wgu_copy.wait()
    wd_copy.wait()
    expert(0)
    from_x(3)
    to_core(1)
    cache_pick()
    from_x(2)
    chip_sum(0)
    expert(1)
    to_core(3)
    chip_sum(1)
    expert(3)
    cache_merge()
    to_core(2)
    chip_sum(3)
    expert_out(0)
    expert(2)
    expert_out(1)
    cache_tp()
    chip_sum(2)
    expert_out(3)
    cache_core()
    expert_out(2)
    attention()

    for e in (1, 3, 2):
        copies.arrived(("r_x", e))
    wide = selw[...]
    high = wide.astype(jnp.bfloat16)
    low = (wide - high.astype(jnp.float32)).astype(jnp.bfloat16)
    joined = bbuf[...].reshape(NX * 64, QF)
    contract = (((0,), (0,)), ((), ()))
    summed = lax.dot_general(high, joined, contract, preferred_element_type=jnp.float32)
    summed += lax.dot_general(low, joined, contract, preferred_element_type=jnp.float32)
    zsend[...] = summed.astype(jnp.bfloat16)
    for d in far_first:
        copies.start(("z", d), zsend.at[pl.ds(d * ROWS, ROWS)], zrecv.at[d], at_z(NZ - d))
    total = summed[0:ROWS]
    for d in far_first:
        copies.arrived(("z", d))
        total += zrecv[d].astype(jnp.float32)
    moe_ref[...] = total.astype(jnp.bfloat16)
    copies.finish()


def routing(expert_ids, gate_weights):
    hot = expert_ids[:, :, None] == jnp.arange(64, dtype=jnp.int32)[None, None, :]
    named = jnp.any(hot, axis=1)
    weight = jnp.sum(jnp.where(hot, gate_weights[:, :, None], 0.0), axis=1)
    named_f = named.astype(jnp.float32)
    earlier = jnp.tril(jnp.ones((ROWS, ROWS), jnp.float32), -1)
    rank = jnp.sum(earlier[:, :, None] * named_f[None, :, :], axis=1)
    code = jnp.where(named, rank, -1.0)

    def by_plane(v):
        return v.reshape(ROWS, NX, NZ, 2).transpose(0, 2, 1, 3).reshape(ROWS, 64)

    return jnp.concatenate([by_plane(code), by_plane(weight)], axis=1)


def body(
    tokens,
    expert_ids,
    gate_weights,
    expert_gate_up,
    expert_down,
    queries,
    latent_cache,
    block_source,
    block_request,
    block_used,
):
    x, z, yh, yl, c = place()
    group = lax.rem(yl + yh, 2) * 2 + c
    meta = routing(expert_ids, gate_weights)

    pieces = lax.dynamic_slice_in_dim(latent_cache, group * 4, 4, axis=1)
    pieces = jnp.pad(pieces.transpose(1, 0, 2), ((0, 0), (0, 0), (0, 640 - LAT)))

    wanted = lax.dynamic_index_in_dim(
        block_source.reshape(NX, NZ, 2, SLOTS), yh, axis=2, keepdims=False
    ).reshape(-1)
    owner = wanted // SLOTS
    place_of = (
        ((owner + yh) % 2) * NZ + (z + NZ - (owner // 2) % NZ) % NZ
    ) * SLOTS + wanted % SLOTS
    place_of = jnp.where(owner // 16 == x, place_of, -1)
    place_of = jnp.broadcast_to(place_of[:, None], (NX * NZ * SLOTS, 128))

    mine = block_request[None, :] == jnp.arange(ROWS, dtype=jnp.int32)[:, None]
    within = jnp.arange(BLK, dtype=jnp.int32)[:, None] < block_used[None, :]
    mask = (mine[:, None, :] & within[None, :, :]).astype(jnp.float32)
    mask = mask.reshape(ROWS, BLK * SLOTS)

    gate_up = expert_gate_up[0].reshape(D, 2 * HID)

    bf16, f32 = jnp.bfloat16, jnp.float32
    vmem = pl.BlockSpec(memory_space=pltpu.VMEM)
    anyspace = pl.BlockSpec(memory_space=pl.ANY)
    count = 96
    moe, attended = pl.pallas_call(
        kernel,
        out_shape=(
            jax.ShapeDtypeStruct((ROWS, QF), bf16),
            jax.ShapeDtypeStruct((256, KV), bf16),
        ),
        in_specs=[vmem] * 6 + [anyspace] * 2,
        out_specs=(vmem, vmem),
        scratch_shapes=[
            pltpu.SemaphoreType.DMA((count,)),
            pltpu.SemaphoreType.DMA((count,)),
            pltpu.SemaphoreType.DMA((4,)),
            pltpu.VMEM((D, 2 * HID), bf16),
            pltpu.VMEM((D, HID), bf16),
            pltpu.VMEM((NZ, ROWS, 128), f32),
            pltpu.VMEM((128, 128), f32),
            pltpu.VMEM((NZ * ROWS, QF), bf16),
            pltpu.VMEM((256, 128), f32),
            pltpu.VMEM((NX, 64, QF), bf16),
            pltpu.VMEM((4, 256, QF), bf16),
            pltpu.VMEM((NX, 32, QF), bf16),
            pltpu.VMEM((NX, 2, 2, 64, QF), bf16),
            pltpu.VMEM((NX, 2, 64, QF), bf16),
            pltpu.VMEM((NX, 2, 64, QF), bf16),
            pltpu.VMEM((NX, 3, 32, QF), bf16),
            pltpu.VMEM((NX, 64, QF), bf16),
            pltpu.VMEM((NX, 64, QF), bf16),
            pltpu.VMEM((NZ * ROWS, QF), bf16),
            pltpu.VMEM((NZ, ROWS, QF), bf16),
            pltpu.VMEM((2 * NZ * SLOTS, PART), bf16),
            pltpu.VMEM((NX, NZ * SLOTS, PART), bf16),
            pltpu.VMEM((NX, NZ * SLOTS, PART), bf16),
            pltpu.VMEM((NZ * SLOTS, PART), bf16),
            pltpu.VMEM((2, 2, 4, SLOTS, KL), bf16),
            pltpu.VMEM((256, KL), bf16),
        ],
        compiler_params=pltpu.CompilerParams(
            collective_id=0, has_side_effects=True, vmem_limit_bytes=56 * 2**20
        ),
        cost_estimate=pl.CostEstimate(
            flops=4 * 10**9, bytes_accessed=13 * 10**6, transcendentals=3 * 10**5
        ),
        name="layer",
    )(
        meta,
        tokens,
        pieces,
        place_of,
        queries.reshape(256, LAT),
        mask,
        gate_up,
        expert_down[0],
    )
    return moe, attended.reshape(ROWS, 16, KV)


def solution(mesh):
    placed = (
        P("ep", "tp"),
        P("ep", None),
        P("ep", None),
        P("ep", None, None, "tp"),
        P("ep", None, "tp"),
        P("ep", "tp", None),
        P("ep", None, None),
        P(),
        P("ep"),
        P("ep"),
    )
    return jax.shard_map(
        body,
        mesh=mesh,
        in_specs=placed,
        out_specs=(P("ep", "tp"), P("ep", "tp", None)),
        check_vma=False,
    )
```

time: 297 us -> 125 us (0.42)
  blocking collectives: 107 us -> 0 us
  Pallas kernels: 0 us -> 104 us
  waiting for transfers between devices: 95.5 us -> 0 us
  starting transfers between devices: 23 us -> 0 us
  local copies, waits for them, and re-layouts: 37.9 us -> 15.6 us
  matrix products: 15.4 us -> 0 us
  between operations: 14.2 us -> 0.77 us
    pallas_call x0 -> x1, Pallas kernels: none -> 104 us  [body(): pl.pallas_call(kernel, out_shape=(jax.ShapeDtypeStruct((ROWS, QF), bf16),...]
    all_to_all x1 -> x0, blocking collectives: 97.8 us -> none  [body(): lax.all_to_all(outgoing.reshape(ep_size, capacity, -1), 'ep', split_axis=...]
    all_to_all x3 -> x0, waiting for transfers between devices: 95.5 us -> none  [the longest x1 39.4 us: move_blocks(): lax.all_to_all(flat_cache, 'ep', split_axis=1, concat_axis=0, tiled=True)]
    all_to_all x3 -> x0, starting transfers between devices: 22.9 us -> none  [the longest x1 8.32 us: body(): lax.all_to_all(summed.reshape(ep_size, capacity, -1), 'ep', split_axis=0,...]
    reshape x5 -> x3, local copies, waits for them, and re-layouts: 20.3 us -> 0.93 us  [the longest x1 0.81 us: body(): block_source.reshape(NX, NZ, 2, SLOTS)]
    dot_general x6 -> x0, matrix products: 15.4 us -> none  [the longest x1 6.39 us: body(): jnp.einsum('sd,dgf->sgf', slot_rows, expert_gate_up[0], preferred_element...]
    gather x1 -> x0, local copies, waits for them, and re-layouts: 11.1 us -> none  [move_blocks(): ordered = jnp.take(spread, block_source, axis=0)]
    unnamed x16 -> x8, local copies, waits for them, and re-layouts: 2.07 us -> 12 us
  transfers between devices with their start and end apart: 4 -> 0, of which waited for: 3 -> 0; matrix products, arithmetic and copies ran while one was open for 8% -> 0% of each run, Pallas kernels for 0% -> 0%
where the time goes in v1:
time: 125 us; the launch traced here: 124 us
  Pallas kernels  104 us (83%)
  local copies, waits for them, and re-layouts  15.6 us (12%)
  other arithmetic  3.4 us (3%)
    pallas_call x1, Pallas kernels, body(): pl.pallas_call(kernel, out_shape=(jax.ShapeDtypeStruct((ROWS, QF), bf16),...  104 us
    unnamed x8, local copies, waits for them, and re-layouts  12 us

profile of v1, /device:TPU:1, one launch (start us, length us, event | category | flops | bytes accessed | tf_op | source)
XLA Modules:
  0.0 124.2 jit_solution(13963938910113122746)
XLA Ops:
  0.6 0.0 copy-start
  0.7 0.7 iota_compare_fusion.2
  1.4 0.7 iota_compare_fusion.1
  2.1 0.1 lt.51
  2.2 0.1 fusion.13
  2.3 0.8 copy.31
  3.0 0.1 fusion
  3.1 0.1 multiply_reduce_fusion
  3.3 0.8 copy.34
  4.0 0.1 select_reduce_fusion
  4.1 0.1 copy.35
  4.2 0.1 copy.38
  4.3 0.1 copy.32
  4.4 0.1 copy.37
  4.5 0.7 pad_maximum_fusion.meta_ref
  5.2 0.1 and.103
  5.3 0.8 reshape.190
  6.1 0.1 compare_reduce_fusion
  6.2 0.1 ne.108
  6.3 0.1 divide_reduce_fusion
  6.5 0.1 div.65
  6.5 0.1 rem.158
  6.6 0.6 and_convert_fusion.mask_ref
  7.3 0.0 copy-done
  7.3 0.1 constant_dynamic-slice_fusion.1
  7.5 0.7 pad.4.cq_ref
  8.2 1.1 broadcast_in_dim.47.jb_ref
  9.3 7.3 %copy.41 = bf16[896,8,2,256]{3,1,2,0:T(8,128)(2,1)} copy(bf16[896,8,2,256]{3,2,1,0:T(2,128)(2,1)} %bitcast.17) | data formatting | bytes 14680064
  16.7 104.5 %layer.1 = (bf16[16,1792]{1,0:T(8,128)(2,1)}, bf16[256,512]{1,0:T(8,128)(2,1)}) custom-call(f32[16,128]{1,0:T(8,128)} %pad_maximum_fusion.meta_ref, bf16[16,1792]{1,0:T(8,128)(2,1)} %tok_ref.1, bf16[4,48,640]{2,1,0:T(8,128)(2,1)} %pad.4.cq_ref, s32[1536,128]{1,0:T(8,128)} %broadcast_in_dim.47.jb_ref, bf16[256,576]{1,0:T(8,128)(2,1)} %bitcast.26, ...), custom_call_target="tpu_custom_call" | custom-call | flops 4000000000 | bytes 13000000 | tf_op jit(solution)/shard_map/layer/pallas_call | solution.py:447
  121.1 1.4 %copy.46 = bf16[16,1792]{1,0:T(8,128)(2,1)} copy(bf16[16,1792]{1,0:T(8,128)(2,1)} %get-tuple-element.10) | data formatting | bytes 114688
  122.6 1.7 %copy.47 = bf16[16,16,512]{2,1,0:T(8,128)(2,1)} copy(bf16[16,16,512]{2,1,0:T(8,128)(2,1)} %bitcast.20) | data formatting | bytes 524288
  (8 shorter events, 0.1 us)
Async XLA Ops:
  0.6 6.7 %copy-start = (bf16[48,16,576]{2,1,0:T(8,128)(2,1)S(1)}, bf16[48,16,576]{2,1,0:T(8,128)(2,1)}, u32[]{:S(2)}) copy-start(bf16[48,16,576]{2,1,0:T(8,128)(2,1)} %param.16) | copy-start | bytes 2654212

commit v2 on v0

v2 whole, which is shorter than its diff:
```python
import jax
import jax.numpy as jnp
from jax import lax
from jax.experimental import pallas as pl
from jax.experimental.pallas import tpu as pltpu
from jax.sharding import PartitionSpec as P

MESH = pl.DeviceIdType.MESH

D = 7168
QF = 1792
HID = 256
ROWS = 16
NX, NZ = 4, 8
SLOTS = 48
HALF = NZ * SLOTS
BLK = 16
LAT = 576
KV = 512
PIECES = 3
KL = 2 * PIECES * 128
TOK = SLOTS * BLK
OFFSETS = (0, 1, 3, 2)
ALONG_Z = (4, 3, 5, 2, 6, 1, 7)
WIDTHS = (384, 640, 768)
STARTS = (0, 384, 1024)
CHUNK = 256

score_scale = 192.0 ** (-0.5)


def place():
    ep, tp = lax.axis_index("ep"), lax.axis_index("tp")
    x = lax.div(ep, 16)
    z = lax.rem(lax.div(ep, 2), NZ)
    return x, z, lax.rem(ep, 2), lax.div(tp, 2), lax.rem(tp, 2)


def device(x, z, yh, yl, c):
    return ((x * NZ + z) * 2 + yh, yl * 2 + c)


def iota(shape, axis):
    return lax.broadcasted_iota(jnp.int32, shape, axis)


def one_hot(equal):
    return jnp.where(equal, 1.0, 0.0).astype(jnp.bfloat16)


def over(values, divisor):
    return jnp.floor((values + 0.5) * (1.0 / divisor))


def dot(a, b):
    return jnp.dot(a, b, preferred_element_type=jnp.float32)


class Copies:
    def __init__(self, send, recv):
        self.send, self.recv, self.made, self.count = send, recv, {}, 0

    def start(self, name, src, dst, to):
        i = self.count
        self.count += 1
        copy = pltpu.make_async_remote_copy(
            src_ref=src,
            dst_ref=dst,
            send_sem=self.send.at[i],
            recv_sem=self.recv.at[i],
            device_id=to,
            device_id_type=MESH,
        )
        copy.start()
        self.made[name] = copy

    def arrived(self, name):
        self.made[name].wait_recv()

    def finish(self):
        for copy in self.made.values():
            copy.wait_send()


def kernel(
    ids_ref,
    gate_ref,
    tok_ref,
    cache_ref,
    source_ref,
    q_ref,
    request_ref,
    used_ref,
    wgu_ref,
    wd_ref,
    moe_ref,
    att_ref,
    send_sem,
    recv_sem,
    local_sem,
    raw,
    wgu,
    wd,
    perm,
    meta,
    metag,
    rows,
    pick,
    selw,
    xsend,
    slots,
    other,
    both,
    hidden,
    part,
    mate,
    chip,
    back,
    ebuf,
    bbuf,
    zsend,
    zrecv,
    cq,
    pos,
    jb,
    cz,
    hots,
    cxs,
    cxr,
    cm,
    keys,
    qp,
):
    x, z, yh, yl, c = place()
    tp = yl * 2 + c
    near_tp = (1 - yl) * 2 + c
    group = lax.rem(yl + yh, 2)
    copies = Copies(send_sem, recv_sem)

    def at_x(e):
        return device(lax.rem(x + e, NX), z, yh, yl, c)

    def at_z(d):
        return device(x, lax.rem(z + d, NZ), yh, yl, c)

    core = device(x, z, yh, yl, 1 - c)
    near = device(x, z, yh, 1 - yl, c)
    cross = device(x, z, 1 - yh, 1 - yl, c)
    far = device(x, z, 1 - yh, yl, c)

    barrier = pltpu.get_barrier_semaphore()
    partners = [at_x(e) for e in range(1, NX)] + [at_z(d) for d in range(1, NZ)]
    partners += [core, near, cross, far]
    for partner in partners:
        pl.semaphore_signal(barrier, inc=1, device_id=partner, device_id_type=MESH)

    raw_copy = pltpu.make_async_copy(wgu_ref, raw, local_sem.at[0])
    wd_copy = pltpu.make_async_copy(wd_ref, wd, local_sem.at[1])
    raw_copy.start()
    wd_copy.start()

    meta[...] = jnp.zeros_like(meta)
    meta[0:8, 0:ROWS] = ids_ref[...].astype(jnp.float32)
    meta[8:16, 0:ROWS] = gate_ref[...]
    to_lanes = jnp.where(iota((128, 128), 1) == iota((128, 128), 0) + z * ROWS, 1.0, 0.0)
    meta[...] = jnp.dot(
        meta[...],
        to_lanes,
        precision=lax.Precision.HIGHEST,
        preferred_element_type=jnp.float32,
    )
    metag[0] = meta[...]
    own_z = pl.ds(pl.multiple_of(z * ROWS, ROWS), ROWS)
    rows[own_z, :] = tok_ref[...]
    pl.semaphore_wait(barrier, len(partners))

    def lanes(f):
        return pl.ds(STARTS[f], WIDTHS[f])

    def send_tables():
        for d in ALONG_Z:
            copies.start(("meta", d), meta, metag.at[d], at_z(d))

    def send_rows(f):
        for d in ALONG_Z:
            copies.start(
                ("tok", f, d), tok_ref.at[:, lanes(f)], rows.at[own_z, lanes(f)], at_z(d)
            )

    send_tables()
    send_rows(0)

    flat = cache_ref[...].reshape(TOK, LAT)
    cq[...] = jnp.zeros_like(cq)
    for t in range(4):
        first = (group * 2 + c) * 4 + t
        hot = one_hot(iota((SLOTS, TOK), 1) == iota((SLOTS, TOK), 0) * BLK + first)
        cq[t, :, 0:LAT] = dot(hot, flat).astype(jnp.bfloat16)

    def piece(d, i):
        to = lax.rem(z + d, NZ)
        lane = pl.multiple_of(lax.rem(to, 2) * 256 + i * 128, 128)
        return cq.at[lax.div(to, 2), :, pl.ds(lane, 128)]

    def own_cz(i):
        return cz.at[i, pl.ds(pl.multiple_of(z * SLOTS, 16), SLOTS)]

    own_pieces = [
        pltpu.make_async_copy(piece(0, i), own_cz(i), local_sem.at[2 + i]) for i in range(PIECES)
    ]
    def send_pieces(i):
        own_pieces[i].start()
        for d in ALONG_Z:
            copies.start(("cz", i, d), piece(d, i), own_cz(i), at_z(d))

    send_rows(1)
    send_pieces(0)
    send_pieces(1)
    send_pieces(2)
    send_rows(2)

    at_row, at_lane = iota((2 * CHUNK, 2 * CHUNK), 0), iota((2 * CHUNK, 2 * CHUNK), 1)
    wanted = jnp.where(at_row < CHUNK, 2 * at_row, 2 * at_row - (2 * CHUNK - 1))
    perm[...] = one_hot(at_lane == wanted)

    def lay_out(first, last):
        @pl.loop(first, last)
        def step(k):
            at = pl.ds(pl.multiple_of(k * CHUNK, CHUNK), CHUNK)
            mixed = raw[at].reshape(2 * CHUNK, HID)
            apart = dot(perm[...], mixed).astype(jnp.bfloat16)
            wgu[at, 0:HID] = apart[:CHUNK]
            wgu[at, HID : 2 * HID] = apart[CHUNK:]

    src = source_ref[...].astype(jnp.float32)
    owner = over(src, SLOTS)
    src_x = over(owner, 16)
    in_x = owner - 16.0 * src_x
    src_z = over(in_x, 2)
    src_y = in_x - 2.0 * src_z
    other_y = jnp.abs(src_y - yh.astype(jnp.float32))
    at = (other_y * NZ + src_z) * SLOTS + (src - owner * SLOTS)
    pos[...] = jnp.where(src_x == x.astype(jnp.float32), at, -1.0)

    for d in ALONG_Z:
        copies.arrived(("meta", d))
    everyone = metag[0]
    for d in ALONG_Z:
        everyone = everyone + metag[d]
    ids, gates = everyone[0:8], everyone[8:16]
    hits, weights = [], []
    for e in OFFSETS:
        for rel in range(2):
            expert = (lax.rem(x + e, NX) * NZ + z) * 2 + (yh if rel == 0 else 1 - yh)
            equal = ids == expert.astype(jnp.float32)
            hits.append(jnp.max(jnp.where(equal, 1.0, 0.0), axis=0, keepdims=True))
            weights.append(jnp.sum(jnp.where(equal, gates, 0.0), axis=0, keepdims=True))
    hit = jnp.concatenate(hits, axis=0)
    before, after = iota((128, 128), 0), iota((128, 128), 1)
    earlier = one_hot(
        (lax.shift_right_logical(before, 4) == lax.shift_right_logical(after, 4))
        & (before < after)
    )
    rank = jnp.where(hit > 0.0, dot(hit.astype(jnp.bfloat16), earlier), -1.0)
    slot_at, row_at = iota((32, 128), 0), iota((32, 128), 1)
    same_source = lax.shift_right_logical(slot_at, 2) == lax.shift_right_logical(row_at, 4)
    slot_rank = lax.bitwise_and(slot_at, 3).astype(jnp.float32)
    for i in range(8):
        hot = same_source & (slot_rank == rank[i : i + 1])
        pick[i * 32 : i * 32 + 32] = one_hot(hot)
        selw[i * 32 : i * 32 + 32] = jnp.where(hot, weights[i], 0.0)

    def from_z(f):
        for d in ALONG_Z:
            copies.arrived(("tok", f, d))
        at = lanes(f)
        picked = dot(pick[...], rows[:, at]).astype(jnp.bfloat16)
        slots[tp, 0:32, at] = picked[0:32]
        other[0:32, at] = picked[32:64]
        along_y(f, 0, 32)
        xsend[:, at] = picked
        for p in (1, 2, 3):
            to, into = at_x(OFFSETS[p]), pl.ds(p * 32, 32)
            low, high = pl.ds(p * 64, 32), pl.ds(p * 64 + 32, 32)
            copies.start(("x0", f, p), xsend.at[low, at], slots.at[tp, into, at], to)
            copies.start(("x1", f, p), xsend.at[high, at], other.at[into, at], to)

    def along_y(f, first, count):
        at, low, high = lanes(f), pl.ds(first, count), pl.ds(128 + first, count)
        copies.start(
            ("near", f, first), slots.at[tp, low, at], slots.at[tp, low, at], near
        )
        copies.start(("cross", f, first), other.at[low, at], slots.at[tp, high, at], cross)
        copies.start(("far", f, first), other.at[low, at], slots.at[tp, high, at], far)

    def from_x(f):
        for p in (1, 2, 3):
            copies.arrived(("x0", f, p))
            copies.arrived(("x1", f, p))
        along_y(f, 32, 96)

    def from_y(f):
        at = lanes(f)
        for first in (0, 32):
            copies.arrived(("near", f, first))
            copies.arrived(("cross", f, first))
        copies.start(("core_n", f), slots.at[near_tp, :, at], slots.at[near_tp, :, at], core)
        for first in (0, 32):
            copies.arrived(("far", f, first))
        copies.start(("core_o", f), slots.at[tp, :, at], slots.at[tp, :, at], core)

    def gate_up(f):
        copies.arrived(("core_n", f))
        copies.arrived(("core_o", f))

        for k in range(4):
            more = dot(
                slots[k, :, lanes(f)], wgu[k * QF + STARTS[f] : k * QF + STARTS[f] + WIDTHS[f], :]
            )
            both[...] = more if f == 0 and k == 0 else both[...] + more

    def activate():
        gate, up = both[:, :HID], both[:, HID:]
        hidden[...] = (gate / (1.0 + jnp.exp(-gate)) * up).astype(jnp.bfloat16)

    def down(f):
        at = lanes(f)

        @pl.loop(0, 4)
        def step(k):
            row = pl.multiple_of(k * QF + STARTS[f], 128)
            part[lax.rem(k, 2), lax.div(k, 2), :, at] = lax.dot_general(
                hidden[...],
                wd[pl.ds(row, WIDTHS[f]), :],
                (((1,), (1,)), ((), ())),
                preferred_element_type=jnp.float32,
            ).astype(jnp.bfloat16)

        copies.start(("mate", f), part.at[1 - c, :, :, at], mate.at[:, :, at], core)

    def chip_sum(f):
        at = lanes(f)
        copies.arrived(("mate", f))
        for h in range(2):
            chip[h, :, at] = (
                part[c, h, :, at].astype(jnp.float32) + mate[h, :, at].astype(jnp.float32)
            ).astype(jnp.bfloat16)
        low, high = pl.ds(0, 128), pl.ds(128, 128)
        copies.start(("r_near", f), chip.at[1 - yl, low, at], back.at[0, :, at], near)
        copies.start(("r_cross", f), chip.at[1 - yl, high, at], back.at[1, :, at], cross)
        copies.start(("r_far", f), chip.at[yl, high, at], back.at[2, :, at], far)

    def expert_out(f):
        at = lanes(f)
        copies.arrived(("r_near", f))
        own = (
            chip[yl, 0:128, at].astype(jnp.float32) + back[0, :, at].astype(jnp.float32)
        ).astype(jnp.bfloat16)
        copies.arrived(("r_cross", f))
        copies.arrived(("r_far", f))
        rest = (
            back[1, :, at].astype(jnp.float32) + back[2, :, at].astype(jnp.float32)
        ).astype(jnp.bfloat16)
        for p in (1, 2, 3, 0):
            into = bbuf if p == 0 else ebuf
            into[p * 64 : p * 64 + 32, at] = own[p * 32 : p * 32 + 32]
            into[p * 64 + 32 : p * 64 + 64, at] = rest[p * 32 : p * 32 + 32]
            if p != 0:
                there = pl.ds(p * 64, 64)
                copies.start(
                    ("r_x", f, p), ebuf.at[there, at], bbuf.at[there, at], at_x(NX - OFFSETS[p])
                )

    def combine(f):
        at = lanes(f)
        for p in (1, 2, 3):
            copies.arrived(("r_x", f, p))
        wide = selw[...]
        high = wide.astype(jnp.bfloat16)
        low = (wide - high.astype(jnp.float32)).astype(jnp.bfloat16)
        contract = (((0,), (0,)), ((), ()))
        joined = bbuf[:, at]
        summed = lax.dot_general(high, joined, contract, preferred_element_type=jnp.float32)
        summed += lax.dot_general(low, joined, contract, preferred_element_type=jnp.float32)
        zsend[:, at] = summed.astype(jnp.bfloat16)
        for d in ALONG_Z:
            there = pl.ds(pl.multiple_of(lax.rem(z + NZ - d, NZ) * ROWS, ROWS), ROWS)
            copies.start(("z", f, d), zsend.at[there, at], zrecv.at[d, :, at], at_z(NZ - d))

    def total(f):
        at = lanes(f)
        out = zsend[own_z, at].astype(jnp.float32)
        for d in ALONG_Z:
            copies.arrived(("z", f, d))
            out += zrecv[d, :, at].astype(jnp.float32)
        moe_ref[:, at] = out.astype(jnp.bfloat16)

    def cache_swap(i):
        own_pieces[i].wait()
        for d in ALONG_Z:
            copies.arrived(("cz", i, d))
        first, second = pl.ds(0, HALF), pl.ds(HALF, HALF)
        copies.start(("swap", i), cz.at[i, first], cz.at[i, second], cross)

    def cache_hot(e):
        lane = iota((HALF, 128), 1).astype(jnp.float32)
        to = lax.rem(x + e, NX)
        for m in range(6):
            line = pos[pl.ds(to * 6 + m, 1), :]
            jb[m * 128 : m * 128 + 128] = jnp.broadcast_to(line, (128, 128)).T
        wants = jnp.concatenate(
            [jb[pl.ds(pl.multiple_of(i * 96 + yh * SLOTS, 16), SLOTS), :] for i in range(NZ)],
            axis=0,
        )
        for k in range(6):
            hots[e, :, k * 128 : k * 128 + 128] = one_hot(wants == lane + 128.0 * k)

    def cache_pick(i):
        copies.arrived(("swap", i))
        for e in (2, 1, 3, 0):
            found = dot(hots[e], cz[i]).astype(jnp.bfloat16)
            if e == 0:
                cxr[0, i] = found
            else:
                cxs[e, i] = found
                copies.start(("cx", i, e), cxs.at[e, i], cxr.at[e, i], at_x(e))

    def own_slots(i, d):
        start = pl.multiple_of(lax.rem(z + d, NZ) * SLOTS, 16)
        return cm.at[i, pl.ds(start, SLOTS)]

    def landing(i):
        lane = pl.multiple_of(lax.rem(z, 2) * 128 + i * 256, 128)
        return keys.at[group, c, lax.div(z, 2), :, pl.ds(lane, 128)]

    own_keys = {}

    def cache_merge(i):
        for e in (1, 3, 2):
            copies.arrived(("cx", i, e))
        cm[i] = (cxr[0, i] + cxr[1, i]) + (cxr[2, i] + cxr[3, i])
        own_keys[i] = pltpu.make_async_copy(
            own_slots(i, 0), landing(i), local_sem.at[2 + PIECES + i]
        )
        own_keys[i].start()
        for d in ALONG_Z:
            copies.start(("k", i, d), own_slots(i, d), landing(i), at_z(d))

    def key_lanes(i):
        return pl.ds(i * 256, 256) if i + 1 < PIECES else pl.ds(KL - 128, 128)

    def cache_tp(i):
        own_keys[i].wait()
        for d in ALONG_Z:
            copies.arrived(("k", i, d))
        there = keys.at[group, c, :, :, key_lanes(i)]
        copies.start(("k_near", i), there, there, near)
        copies.start(("k_core", i, 0), there, there, core)

    def cache_core(i):
        copies.arrived(("k_near", i))
        there = keys.at[1 - group, c, :, :, key_lanes(i)]
        copies.start(("k_core", i, 1), there, there, core)

    def place_queries():
        qp[...] = jnp.zeros_like(qp)
        flat_q = q_ref[...].reshape(256, LAT)
        for i in range(2):
            for h in range(2):
                entry, lane = h * 256 + i * 128, i * 256 + h * 128
                qp[:, lane : lane + 128] = flat_q[:, entry : entry + 128]
        qp[:, 640 : 640 + LAT - KV] = flat_q[:, KV:LAT]

    def attention():
        for i in range(PIECES):
            copies.arrived(("k_core", i, 0))
            copies.arrived(("k_core", i, 1))
        held = keys[...].reshape(TOK, KL)
        rows_with_rows = (((1,), (1,)), ((), ()))
        scores = lax.dot_general(
            qp[:, 0:KV], held[:, 0:KV], rows_with_rows, preferred_element_type=jnp.float32
        )
        scores += lax.dot_general(
            qp[:, KL - 128 : KL],
            held[:, KL - 128 : KL],
            rows_with_rows,
            preferred_element_type=jnp.float32,
        )
        scores *= score_scale
        at = iota((SLOTS, TOK), 1).astype(jnp.float32)
        token = over(at, SLOTS)
        spread = one_hot(at - token * SLOTS == iota((SLOTS, TOK), 0).astype(jnp.float32))
        numbers = jnp.concatenate(
            [
                jnp.broadcast_to(request_ref[...].astype(jnp.float32), (8, SLOTS)),
                jnp.broadcast_to(used_ref[...].astype(jnp.float32), (8, SLOTS)),
            ],
            axis=0,
        ).astype(jnp.bfloat16)
        told = dot(numbers, spread)
        request, used = told[0:1], told[8:9]
        request = jnp.where(token[0:1] < used, request, -1.0)
        row = lax.shift_right_logical(iota((256, TOK), 0), 4).astype(jnp.float32)
        scores = jnp.where(row == request, scores, -1e30)
        terms = jnp.exp(scores - jnp.max(scores, axis=1, keepdims=True))
        weights = (terms / jnp.sum(terms, axis=1, keepdims=True)).astype(jnp.bfloat16)
        attended = dot(weights, held[:, 0:KV]).astype(jnp.bfloat16)
        for i in range(2):
            for h in range(2):
                entry, lane = h * 256 + i * 128, i * 256 + h * 128
                att_ref[:, entry : entry + 128] = attended[:, lane : lane + 128]

    from_z(0)
    cache_hot(2)
    cache_hot(1)
    raw_copy.wait()
    from_x(0)
    from_z(1)
    cache_hot(3)
    cache_swap(0)
    cache_hot(0)
    from_x(1)
    cache_swap(1)
    from_z(2)
    cache_swap(2)
    lay_out(0, 8)
    from_x(2)
    lay_out(8, 14)
    from_y(0)
    cache_pick(0)
    cache_pick(1)
    cache_pick(2)
    lay_out(14, 22)
    from_y(1)
    lay_out(22, 28)
    gate_up(0)
    gate_up(1)
    from_y(2)
    wd_copy.wait()
    place_queries()
    gate_up(2)
    activate()
    down(2)
    down(1)
    chip_sum(2)
    down(0)
    chip_sum(1)
    chip_sum(0)
    cache_merge(0)
    cache_merge(1)
    cache_merge(2)
    expert_out(2)
    cache_tp(0)
    expert_out(1)
    cache_tp(1)
    combine(2)
    cache_tp(2)
    expert_out(0)
    cache_core(0)
    cache_core(1)
    combine(1)
    cache_core(2)
    attention()
    combine(0)
    total(2)
    total(1)
    total(0)
    copies.finish()


def hand_out(moe_ref, att_ref, moe_out, att_out):
    moe_out[...] = moe_ref[...]
    att_out[...] = att_ref[...]


def body(
    tokens,
    expert_ids,
    gate_weights,
    expert_gate_up,
    expert_down,
    queries,
    latent_cache,
    block_source,
    block_request,
    block_used,
):
    bf16, f32 = jnp.bfloat16, jnp.float32
    vmem = pl.BlockSpec(memory_space=pltpu.VMEM)
    anyspace = pl.BlockSpec(memory_space=pl.ANY)
    count = 7 + 3 * 37 + 63
    results = (
        jax.ShapeDtypeStruct((ROWS, QF), bf16),
        jax.ShapeDtypeStruct((256, KV), bf16),
    )
    moe, attended = pl.pallas_call(
        kernel,
        out_shape=results,
        in_specs=[vmem] * 8 + [anyspace] * 2,
        out_specs=(vmem, vmem),
        scratch_shapes=[
            pltpu.SemaphoreType.DMA((count,)),
            pltpu.SemaphoreType.DMA((count,)),
            pltpu.SemaphoreType.DMA((8,)),
            pltpu.VMEM((D, 2, HID), bf16),
            pltpu.VMEM((D, 2 * HID), bf16),
            pltpu.VMEM((D, HID), bf16),
            pltpu.VMEM((2 * CHUNK, 2 * CHUNK), bf16),
            pltpu.VMEM((16, 128), f32),
            pltpu.VMEM((NZ, 16, 128), f32),
            pltpu.VMEM((NZ * ROWS, QF), bf16),
            pltpu.VMEM((256, 128), bf16),
            pltpu.VMEM((256, 128), f32),
            pltpu.VMEM((256, QF), bf16),
            pltpu.VMEM((4, 256, QF), bf16),
            pltpu.VMEM((128, QF), bf16),
            pltpu.VMEM((256, 2 * HID), f32),
            pltpu.VMEM((256, HID), bf16),
            pltpu.VMEM((2, 2, 256, QF), bf16),
            pltpu.VMEM((2, 256, QF), bf16),
            pltpu.VMEM((2, 256, QF), bf16),
            pltpu.VMEM((3, 128, QF), bf16),
            pltpu.VMEM((256, QF), bf16),
            pltpu.VMEM((256, QF), bf16),
            pltpu.VMEM((NZ * ROWS, QF), bf16),
            pltpu.VMEM((NZ, ROWS, QF), bf16),
            pltpu.VMEM((4, SLOTS, 640), bf16),
            pltpu.VMEM((24, 128), f32),
            pltpu.VMEM((TOK, 128), f32),
            pltpu.VMEM((PIECES, 2 * HALF, 128), bf16),
            pltpu.VMEM((NX, HALF, 2 * HALF), bf16),
            pltpu.VMEM((NX, PIECES, HALF, 128), bf16),
            pltpu.VMEM((NX, PIECES, HALF, 128), bf16),
            pltpu.VMEM((PIECES, HALF, 128), bf16),
            pltpu.VMEM((2, 2, 4, SLOTS, KL), bf16),
            pltpu.VMEM((256, KL), bf16),
        ],
        compiler_params=pltpu.CompilerParams(
            collective_id=0, has_side_effects=True, vmem_limit_bytes=56 * 2**20
        ),
        cost_estimate=pl.CostEstimate(
            flops=8 * 10**9, bytes_accessed=13 * 10**6, transcendentals=3 * 10**5
        ),
        name="layer",
    )(
        expert_ids.T,
        gate_weights.T,
        tokens,
        latent_cache,
        block_source.reshape(24, 128),
        queries,
        block_request.reshape(1, SLOTS),
        block_used.reshape(1, SLOTS),
        expert_gate_up[0],
        expert_down[0],
    )
    moe, attended = pl.pallas_call(
        hand_out, out_shape=results, in_specs=[vmem] * 2, out_specs=(vmem, vmem), name="results"
    )(moe, attended)
    return moe, attended.reshape(ROWS, 16, KV)


def solution(mesh):
    placed = (
        P("ep", "tp"),
        P("ep", None),
        P("ep", None),
        P("ep", None, None, "tp"),
        P("ep", None, "tp"),
        P("ep", "tp", None),
        P("ep", None, None),
        P(),
        P("ep"),
        P("ep"),
    )
    return jax.shard_map(
        body,
        mesh=mesh,
        in_specs=placed,
        out_specs=(P("ep", "tp"), P("ep", "tp", None)),
        check_vma=False,
    )
```

time: 297 us -> 102 us (0.34)
  blocking collectives: 107 us -> 0 us
  Pallas kernels: 0 us -> 101 us
  waiting for transfers between devices: 95.5 us -> 0 us
  local copies, waits for them, and re-layouts: 37.9 us -> 0 us
  starting transfers between devices: 23 us -> 0 us
  matrix products: 15.4 us -> 0 us
  between operations: 14.2 us -> 0.64 us
    pallas_call x0 -> x2, Pallas kernels: none -> 101 us  [the longest x1 99.1 us: body(): pl.pallas_call(kernel, out_shape=results, in_specs=[vmem] * 8 + [anyspace...]
    all_to_all x1 -> x0, blocking collectives: 97.8 us -> none  [body(): lax.all_to_all(outgoing.reshape(ep_size, capacity, -1), 'ep', split_axis=...]
    all_to_all x3 -> x0, waiting for transfers between devices: 95.5 us -> none  [the longest x1 39.4 us: move_blocks(): lax.all_to_all(flat_cache, 'ep', split_axis=1, concat_axis=0, tiled=True)]
    all_to_all x3 -> x0, starting transfers between devices: 22.9 us -> none  [the longest x1 8.32 us: body(): lax.all_to_all(summed.reshape(ep_size, capacity, -1), 'ep', split_axis=0,...]
    reshape x5 -> x0, local copies, waits for them, and re-layouts: 20.3 us -> none  [the longest x1 7 us: body(): outgoing.reshape(ep_size, capacity, -1)]
    dot_general x6 -> x0, matrix products: 15.4 us -> none  [the longest x1 6.39 us: body(): jnp.einsum('sd,dgf->sgf', slot_rows, expert_gate_up[0], preferred_element...]
    gather x1 -> x0, local copies, waits for them, and re-layouts: 11.1 us -> none  [move_blocks(): ordered = jnp.take(spread, block_source, axis=0)]
    all_gather x1 -> x0, blocking collectives: 8.98 us -> none  [body(): full_rows = lax.all_gather(tokens, 'tp', axis=1, tiled=True)]
  transfers between devices with their start and end apart: 4 -> 0, of which waited for: 3 -> 0; matrix products, arithmetic and copies ran while one was open for 8% -> 0% of each run, Pallas kernels for 0% -> 0%
where the time goes in v2:
time: 102 us
  Pallas kernels  101 us (99%)
    pallas_call x1, Pallas kernels, body(): pl.pallas_call(kernel, out_shape=results, in_specs=[vmem] * 8 + [anyspace...  99.1 us

profile of v2, /device:TPU:1, one launch (start us, length us, event | category | flops | bytes accessed | tf_op | source)
XLA Modules:
  0.0 101.5 jit_solution(1862051522008841221)
XLA Ops:
  0.6 99.1 %layer.1 = (bf16[16,1792]{1,0:T(8,128)(2,1)}, bf16[256,512]{1,0:T(8,128)(2,1)}) custom-call(s32[8,16]{1,0:T(8,128)} %bitcast.12, f32[8,16]{1,0:T(8,128)} %bitcast.13, bf16[16,1792]{1,0:T(8,128)(2,1)} %tok_ref.1, bf16[48,16,576]{2,1,0:T(8,128)(2,1)} %cache_ref.1, s32[24,128]{1,0:T(8,128)} %bitcast.11, bf16[16,16,576]{2,1,0:T(8,128)(2,1)} %q_ref.1, ...), custom_call_target="tpu_custom_call" | custom-call | flops 8000000000 | bytes 13000000 | tf_op jit(solution)/shard_map/layer/pallas_call | solution.py:596
  99.8 1.7 %results.1 = (bf16[16,1792]{1,0:T(8,128)(2,1)}, bf16[256,512]{1,0:T(8,128)(2,1)}) custom-call(bf16[16,1792]{1,0:T(8,128)(2,1)} %get-tuple-element.6.moe_ref, bf16[256,512]{1,0:T(8,128)(2,1)} %get-tuple-element.7.att_ref), custom_call_target="tpu_custom_call" | custom-call | tf_op jit(solution)/shard_map/results/pallas_call | solution.py:657

commit v3 on v2

--- a/solution.py
+++ b/solution.py
@@ -24,6 +24,7 @@
 ALONG_Z = (4, 3, 5, 2, 6, 1, 7)
 WIDTHS = (384, 640, 768)
 STARTS = (0, 384, 1024)
+OUT_RELAYED = (0, 1,)
 CHUNK = 256
 
 score_scale = 192.0 ** (-0.5)
@@ -291,7 +292,8 @@
             ("near", f, first), slots.at[tp, low, at], slots.at[tp, low, at], near
         )
         copies.start(("cross", f, first), other.at[low, at], slots.at[tp, high, at], cross)
-        copies.start(("far", f, first), other.at[low, at], slots.at[tp, high, at], far)
+        if f not in OUT_RELAYED:
+            copies.start(("far", f, first), other.at[low, at], slots.at[tp, high, at], far)
 
     def from_x(f):
         for p in (1, 2, 3):
@@ -299,14 +301,25 @@
             copies.arrived(("x1", f, p))
         along_y(f, 32, 96)
 
+    def relay(f):
+        at = lanes(f)
+        for first in (0, 32):
+            copies.arrived(("cross", f, first))
+        there = slots.at[near_tp, pl.ds(128, 128), at]
+        copies.start(("relay", f), there, there, near)
+
     def from_y(f):
         at = lanes(f)
         for first in (0, 32):
             copies.arrived(("near", f, first))
-            copies.arrived(("cross", f, first))
+            if f not in OUT_RELAYED:
+                copies.arrived(("cross", f, first))
         copies.start(("core_n", f), slots.at[near_tp, :, at], slots.at[near_tp, :, at], core)
-        for first in (0, 32):
-            copies.arrived(("far", f, first))
+        if f in OUT_RELAYED:
+            copies.arrived(("relay", f))
+        else:
+            for first in (0, 32):
+                copies.arrived(("far", f, first))
         copies.start(("core_o", f), slots.at[tp, :, at], slots.at[tp, :, at], core)
 
     def gate_up(f):
@@ -346,9 +359,9 @@
                 part[c, h, :, at].astype(jnp.float32) + mate[h, :, at].astype(jnp.float32)
             ).astype(jnp.bfloat16)
         low, high = pl.ds(0, 128), pl.ds(128, 128)
-        copies.start(("r_near", f), chip.at[1 - yl, low, at], back.at[0, :, at], near)
         copies.start(("r_cross", f), chip.at[1 - yl, high, at], back.at[1, :, at], cross)
         copies.start(("r_far", f), chip.at[yl, high, at], back.at[2, :, at], far)
+        copies.start(("r_near", f), chip.at[1 - yl, low, at], back.at[0, :, at], near)
 
     def expert_out(f):
         at = lanes(f)
@@ -521,17 +534,19 @@
     cache_hot(0)
     from_x(1)
     cache_swap(1)
+    relay(0)
     from_z(2)
     cache_swap(2)
     lay_out(0, 8)
     from_x(2)
-    lay_out(8, 14)
+    relay(1)
+    lay_out(8, 12)
     from_y(0)
     cache_pick(0)
     cache_pick(1)
+    lay_out(12, 22)
+    from_y(1)
     cache_pick(2)
-    lay_out(14, 22)
-    from_y(1)
     lay_out(22, 28)
     gate_up(0)
     gate_up(1)
@@ -541,27 +556,27 @@
     gate_up(2)
     activate()
     down(2)
+    chip_sum(2)
     down(1)
-    chip_sum(2)
+    chip_sum(1)
     down(0)
-    chip_sum(1)
     chip_sum(0)
     cache_merge(0)
     cache_merge(1)
     cache_merge(2)
     expert_out(2)
+    expert_out(1)
+    combine(2)
     cache_tp(0)
-    expert_out(1)
+    expert_out(0)
     cache_tp(1)
-    combine(2)
+    combine(1)
     cache_tp(2)
-    expert_out(0)
     cache_core(0)
+    combine(0)
     cache_core(1)
-    combine(1)
     cache_core(2)
     attention()
-    combine(0)
     total(2)
     total(1)
     total(0)

time: 102 us -> 94.6 us (0.927)
  Pallas kernels: 101 us -> 92.8 us
    pallas_call x1, Pallas kernels: 99.1 us -> 91.1 us  [body(): pl.pallas_call(kernel, out_shape=results, in_specs=[vmem] * 8 + [anyspace...]
where the time goes in v3:
time: 94.6 us; the launch traced here: 93.5 us
  Pallas kernels  92.8 us (98%)
    pallas_call x1, Pallas kernels, body(): pl.pallas_call(kernel, out_shape=results, in_specs=[vmem] * 8 + [anyspace...  91.1 us

profile of v3, /device:TPU:1, one launch (start us, length us, event | category | flops | bytes accessed | tf_op | source)
XLA Modules:
  0.0 93.5 jit_solution(12204117294345941177)
XLA Ops:
  0.6 91.1 %layer.1 = (bf16[16,1792]{1,0:T(8,128)(2,1)}, bf16[256,512]{1,0:T(8,128)(2,1)}) custom-call(s32[8,16]{1,0:T(8,128)} %bitcast.12, f32[8,16]{1,0:T(8,128)} %bitcast.13, bf16[16,1792]{1,0:T(8,128)(2,1)} %tok_ref.1, bf16[48,16,576]{2,1,0:T(8,128)(2,1)} %cache_ref.1, s32[24,128]{1,0:T(8,128)} %bitcast.11, bf16[16,16,576]{2,1,0:T(8,128)(2,1)} %q_ref.1, ...), custom_call_target="tpu_custom_call" | custom-call | flops 8000000000 | bytes 13000000 | tf_op jit(solution)/shard_map/layer/pallas_call | solution.py:611
  91.8 1.7 %results.1 = (bf16[16,1792]{1,0:T(8,128)(2,1)}, bf16[256,512]{1,0:T(8,128)(2,1)}) custom-call(bf16[16,1792]{1,0:T(8,128)(2,1)} %get-tuple-element.6.moe_ref, bf16[256,512]{1,0:T(8,128)(2,1)} %get-tuple-element.7.att_ref), custom_call_target="tpu_custom_call" | custom-call | tf_op jit(solution)/shard_map/results/pallas_call | solution.py:672

commit v4 on v3

--- a/solution.py
+++ b/solution.py
@@ -22,8 +22,8 @@
 TOK = SLOTS * BLK
 OFFSETS = (0, 1, 3, 2)
 ALONG_Z = (4, 3, 5, 2, 6, 1, 7)
-WIDTHS = (384, 640, 768)
-STARTS = (0, 384, 1024)
+WIDTHS = (384, 768, 640)
+STARTS = (0, 384, 1152)
 OUT_RELAYED = (0, 1,)
 CHUNK = 256
 
@@ -188,8 +188,8 @@
                 ("tok", f, d), tok_ref.at[:, lanes(f)], rows.at[own_z, lanes(f)], at_z(d)
             )
 
+    send_rows(0)
     send_tables()
-    send_rows(0)
 
     flat = cache_ref[...].reshape(TOK, LAT)
     cq[...] = jnp.zeros_like(cq)

time: 94.6 us -> 95.6 us (1.011)
  no operation moved by 1% of the time
where the time goes in v4:
time: 95.6 us; the launch traced here: 94.3 us
  Pallas kernels  93.6 us (98%)
    pallas_call x1, Pallas kernels, body(): pl.pallas_call(kernel, out_shape=results, in_specs=[vmem] * 8 + [anyspace...  91.9 us

profile of v4, /device:TPU:1, one launch (start us, length us, event | category | flops | bytes accessed | tf_op | source)
XLA Modules:
  0.0 94.3 jit_solution(11716565627386905663)
XLA Ops:
  0.6 91.9 %layer.1 = (bf16[16,1792]{1,0:T(8,128)(2,1)}, bf16[256,512]{1,0:T(8,128)(2,1)}) custom-call(s32[8,16]{1,0:T(8,128)} %bitcast.12, f32[8,16]{1,0:T(8,128)} %bitcast.13, bf16[16,1792]{1,0:T(8,128)(2,1)} %tok_ref.1, bf16[48,16,576]{2,1,0:T(8,128)(2,1)} %cache_ref.1, s32[24,128]{1,0:T(8,128)} %bitcast.11, bf16[16,16,576]{2,1,0:T(8,128)(2,1)} %q_ref.1, ...), custom_call_target="tpu_custom_call" | custom-call | flops 8000000000 | bytes 13000000 | tf_op jit(solution)/shard_map/layer/pallas_call | solution.py:611
  92.5 1.7 %results.1 = (bf16[16,1792]{1,0:T(8,128)(2,1)}, bf16[256,512]{1,0:T(8,128)(2,1)}) custom-call(bf16[16,1792]{1,0:T(8,128)(2,1)} %get-tuple-element.6.moe_ref, bf16[256,512]{1,0:T(8,128)(2,1)} %get-tuple-element.7.att_ref), custom_call_target="tpu_custom_call" | custom-call | tf_op jit(solution)/shard_map/results/pallas_call | solution.py:672
